TPU v7x, 1024 devices: a whole 8x8x8 slice. The times are simulated.
1024 devices in a mesh: tm: 64 (over z, y_hi, core), space: 16 (over y_lo, x).
Axes of the slice: x: 8, y: 8 (y_hi: 4, y_lo: 2; y = y_hi * 2 + y_lo), z: 8, core: 2. Of those that a mesh axis runs over, the one named last changes fastest.
Arguments:
- guess: float32 [64, 5, 64, 2048], P('tm', None, None, 'space'), may hold values from -6 to 6
- deriv: float32 [64, 64], replicated, may hold values from -0.75 to 0.75
- viscous: float32 [64, 64], replicated, may hold values from -0.75 to 0.75
- flux_jacobian: float32 [5, 5], replicated, may hold values from -2.5 to 2.5
- upwind: float32 [5, 5], replicated, may hold values from -2.5 to 2.5
- lift: float32 [64, 16], replicated, may hold values from -1.5 to 1.5
- restrict: float32 [8, 64], replicated, may hold values from -0.75 to 0.75
- prolong: float32 [64, 8], replicated, may hold values from -2 to 2
- coarse_self: float32 [40, 40], replicated
- coarse_group: float32 [40, 40], replicated
- neighbors: int32 [2048], P('space'), may hold values from 0 to 2047, as said below
- coarse_map: int32 [2048], replicated, may hold values from 0 to 2047, as said below
Outputs:
- starts: float32 [64, 5, 64, 2048], P('tm', None, None, 'space')
Inputs may be any that keep to these rules, and one draw needn't show every extreme that they name: `neighbors`: the element across the upwind face of an element of partition p (elements p*128 to (p+1)*128 - 1) lies in partition p or in the partition before it, cyclically. `coarse_map`: a permutation of all elements; positions q*128 to (q+1)*128 - 1 take an equal share of elements from every partition, the shares in order of partition.
All inputs are finite; a program needn't handle non-finite values.
Results may differ from a plain program's by a relative error of at most 0.0003.
Values sent between devices are 32-bit elements; how exact they have to be, the bound alone decides.
A program may use at most 32 MiB of HBM per device.

v0:
```python
import functools

import jax
import jax.numpy as jnp
from jax import lax
from jax.experimental import pallas as pl
from jax.experimental.pallas import tpu as pltpu
from jax.sharding import PartitionSpec as P

COMP = 5
NODES = 64
FACE = 16
CNODES = 8
SUB = 8
ITERS = 2
COARSE = 40
EL = 128
WIDE = COMP * EL
NY = 4
NZ = 8
STEP = 0.08

f32 = jnp.float32
bf16 = jnp.bfloat16
highest = lax.Precision.HIGHEST
MESH = pl.DeviceIdType.MESH

HALO = 0
SEM_S = HALO + SUB * ITERS
SEM_F = SEM_S + ITERS
SEM_Y = SEM_F + 2 * ITERS
SEM_Z = SEM_Y + 3 * ITERS
SEM_P = SEM_Z + 7 * ITERS
SEM_Q = SEM_P + ITERS
SEM_END = SEM_Q + 3 * ITERS
SEMS = SEM_END + 1


def iota(shape, dim):
    return lax.broadcasted_iota(jnp.int32, shape, dim)


def dot(a, b):
    return jnp.dot(a, b, preferred_element_type=f32)


def dot32(a, b):
    return jnp.dot(a, b, precision=highest, preferred_element_type=f32)


def halves(x):
    high = x.astype(bf16)
    return high, (x - high.astype(f32)).astype(bf16)


def stack3(x):
    high, low = halves(x)
    return jnp.concatenate([high, high, low], axis=0)


def spread3(x, place):
    depth = x.shape[1]
    rows, cols = iota((depth, 3 * depth), 0), iota((depth, 3 * depth), 1)
    third = cols // depth
    hit = place(rows, cols - third * depth)
    high, low = halves(x)
    outer = jnp.where(hit & (third != 1), 1.0, 0.0).astype(bf16)
    middle = jnp.where(hit & (third == 1), 1.0, 0.0).astype(bf16)
    return (dot(high, outer) + dot(low, middle)).astype(bf16)


def same(row, col):
    return row == col


def node_place(row, col):
    return row == (col % FACE) * 4 + (col // FACE + 3) % 4


def node_rows(ref, start=0):
    return jnp.concatenate(
        [ref[pl.ds(start + i, FACE, stride=4), :] for i in (3, 0, 1, 2)], axis=0
    )


def part(x, c):
    return x[:, c * EL : (c + 1) * EL]


def pick(x, index):
    return jnp.take_along_axis(x, jnp.broadcast_to(index, x.shape), axis=1, mode="promise_in_bounds")


def tall(x):
    return jnp.concatenate([part(x, c) for c in range(COMP)], axis=0)


def wide(x):
    return jnp.concatenate([x[c * CNODES : (c + 1) * CNODES] for c in range(COMP)], axis=1)


def kernel(
    guess, deriv, viscous, jacobian, upwind, lift, restrict, prolong, self_ref, group_ref, neighbors, coarse_map,
    out,
    state, base, sent, landed, s_out, s_in, f_out, f_pair, t_all, z_out, z_all, p_pair, q_out, q_all, cand, fin,
    gen3, lift3, rst3, rl3, w_m, w_y, w_z, w_q, maps,
    ssem, rsem,
):
    tm, sp = lax.axis_index("tm"), lax.axis_index("space")
    core, chip = lax.rem(tm, 2), tm // 2
    yh, z = lax.rem(chip, NY), chip // NY
    slices, parts = 2 * NY * NZ, 16

    def at(t=None, s=None):
        return {"tm": tm if t is None else t, "space": sp if s is None else s}

    def chip_at(q, c):
        return at(2 * lax.rem(q + NY * NZ, NY * NZ) + c)

    def y_at(k):
        return at((z * NY + lax.rem(yh + k + NY, NY)) * 2 + core)

    def z_at(k):
        return at(lax.rem(tm + 2 * NY * k + slices, slices))

    def sp_at(k):
        return at(None, lax.rem(sp + k + parts, parts))

    sibling = at(tm + 1 - 2 * core)
    upper = at(lax.rem(tm + 1, slices))
    lower = at(lax.rem(tm + slices - 1, slices))

    def copy(src, dst, send, recv, to):
        return pltpu.make_async_remote_copy(
            src_ref=src, dst_ref=dst, send_sem=ssem.at[send], recv_sem=rsem.at[recv], device_id=to, device_id_type=MESH
        )

    def halo(n):
        return copy(sent.at[n], landed.at[n], HALO + n, HALO + n, sp_at(1))

    def s_copy(it):
        return copy(s_out.at[it], s_in.at[it], SEM_S + it, SEM_S + it, lower)

    def f_near():
        return copy(f_out.at[0], f_pair.at[0, core], SEM_F, SEM_F, sibling)

    def f_far(c):
        return copy(f_out.at[1], f_pair.at[1, core], SEM_F + 2 + c, SEM_F + 2 + core, chip_at(chip + 1, c))

    def y_copy(it, k):
        return copy(t_all.at[it, yh], t_all.at[it, yh], SEM_Y + 3 * it + k - 1, SEM_Y + 3 * it + k - 1, y_at(k))

    def z_copy(it, k):
        return copy(z_out.at[it], z_all.at[it, k - 1], SEM_Z + 7 * it + k - 1, SEM_Z + 7 * it + k - 1, z_at(k))

    def p_copy(it):
        return copy(p_pair.at[it, core], p_pair.at[it, core], SEM_P + it, SEM_P + it, sibling)

    def q_copy(it, k):
        return copy(q_out.at[it], q_all.at[it, k - 1], SEM_Q + 3 * it + k - 1, SEM_Q + 3 * it + k - 1, sp_at(4 * k))

    z_all[...] = jnp.zeros_like(z_all)
    f_pair[...] = jnp.zeros_like(f_pair)

    barrier = pltpu.get_barrier_semaphore()
    senders = [sp_at(-1), upper, sibling, chip_at(chip - 1, 0), chip_at(chip - 1, 1)]
    senders += [y_at(-k) for k in (1, 2, 3)] + [z_at(-k) for k in range(1, NZ)] + [sp_at(-4 * k) for k in (1, 2, 3)]
    for device in senders:
        pl.semaphore_signal(barrier, inc=1, device_id=device, device_id_type=MESH)

    for c in range(COMP):
        state[:, c * EL : (c + 1) * EL] = node_rows(guess, c * NODES)
    sent[0] = state[0:FACE, :]

    index = neighbors[...] % EL
    own = (neighbors[...] // EL) == jnp.broadcast_to(sp, (1, EL))
    own = jnp.broadcast_to(own, (FACE, EL))

    volume = jnp.concatenate([node_rows(viscous), node_rows(deriv)], axis=0) * STEP
    gen3[...] = spread3(volume, node_place)
    lift_rows = node_rows(lift) * STEP
    lift3[...] = spread3(lift_rows, same)

    pl.semaphore_wait(barrier, len(senders))
    halo(0).start()

    def substep(n, side):
        last = n % SUB == SUB - 1
        v = state[...]
        yz = dot(gen3[...], stack3(v))
        plus, minus = v[0:FACE], v[FACE : 2 * FACE]
        inner = [pick(part(plus, d), index) - part(minus, d) for d in range(COMP)]
        for c in range(COMP):
            total = part(v, c) + part(yz[0:NODES], c)
            for d in range(COMP):
                total = total - jacobian[c, d] * part(yz[NODES:], d)
            base[:, c * EL : (c + 1) * EL] = total
        if last:
            coarse_base = dot(rst3[...], stack3(base[...]))
        side()
        halo(n).wait_recv()
        jump = [jnp.where(own, inner[d], pick(landed[n, :, d * EL : (d + 1) * EL], index) - part(minus, d)) for d in range(COMP)]
        mixed = []
        for c in range(COMP):
            total = upwind[c, 0] * jump[0]
            for d in range(1, COMP):
                total = total + upwind[c, d] * jump[d]
            mixed.append(total)
        faces = stack3(jnp.concatenate(mixed, axis=1))
        if last:
            ends = coarse_base + dot(rl3[...], faces)
            state[...] = base[...] + dot(lift3[...], faces)
            return ends
        trace = base[0:FACE, :] + dot(lift3[0:FACE, :], faces)
        sent[n + 1] = trace
        halo(n + 1).start()
        state[0:FACE, :] = trace
        state[FACE:, :] = base[FACE:, :] + dot(lift3[FACE:, :], faces)

    def send_starts(it):
        s_out[it] = tall(dot(rst3[...], stack3(state[...])))
        s_copy(it).start()

    def restriction():
        full = restrict[...]
        rst3[...] = spread3(full, node_place)
        rows, cols = iota((NODES, NODES), 0), iota((NODES, NODES), 1)
        moved = dot32(full, jnp.where(node_place(rows, cols), 1.0, 0.0))
        rl3[...] = spread3(dot32(moved, lift_rows), same)
        send_starts(0)

    def orders():
        lane = iota((16, EL), 1)
        here = pick(coarse_map[...], sp * 8 + lane % 8)
        chosen = jnp.where(iota((16, EL), 0) == lane // 8, here.astype(f32), 0.0)
        member = jnp.sum(chosen, axis=0, keepdims=True) - jnp.broadcast_to(sp * EL, (1, EL)).astype(f32)
        grid = jnp.transpose(jnp.broadcast_to(member, (EL, EL)))
        hit = grid == iota((EL, EL), 1).astype(f32)
        back = jnp.sum(jnp.where(hit, iota((EL, EL), 0).astype(f32), 0.0), axis=0, keepdims=True)
        maps[0:8] = jnp.broadcast_to(member, (8, EL)).astype(jnp.int32)
        maps[8:16] = jnp.broadcast_to(back, (8, EL)).astype(jnp.int32)

    small = (COARSE, COARSE)
    second = jnp.broadcast_to(core, small) == 1
    eye = jnp.where(iota(small, 0) == iota(small, 1), 1.0, 0.0)
    zero = jnp.zeros(small, f32)

    def powers():
        m = self_ref[...] + jnp.where(second, group_ref[...], 0.0)
        w = dot32(m, m)
        w2 = dot32(w, w)
        w_m[0] = m
        w_m[1] = w
        w_m[2] = w2
        w_m[3] = dot32(w2, w)
        w_m[4] = dot32(w2, w2)

    def beside(blocks):
        count = len(blocks)
        total = None
        for k, block in enumerate(blocks):
            rows, cols = iota((COARSE, COARSE * count), 0), iota((COARSE, COARSE * count), 1)
            term = dot32(block, jnp.where(cols - COARSE * k == rows, 1.0, 0.0))
            total = term if total is None else total + term
        return total

    def by_yh(choices):
        place = jnp.broadcast_to(yh, small)
        value = choices[3]
        for j in (2, 1, 0):
            value = jnp.where(place == j, choices[j], value)
        return value

    def y_weights():
        w, w2, w3 = w_m[1], w_m[2], w_m[3]
        w_y[0:COARSE] = beside(
            [
                by_yh([zero, eye, w, w2]),
                by_yh([zero, zero, eye, w]),
                by_yh([zero, zero, zero, eye]),
                zero,
            ]
        )
        w_y[COARSE:] = beside([w3, w2, w, eye])

    def z_weights():
        w8 = w_m[4]
        weight = by_yh([eye, w_m[1], w_m[2], w_m[3]])
        weights = [weight]
        for k in range(NZ - 2):
            weight = dot32(weight, w8)
            weights.append(weight)
        w_z[...] = beside(weights)

    def q_weights():
        a, group = self_ref[...], group_ref[...]
        b = a + group
        a1 = jnp.where(second, dot32(a, a), a)
        b1 = jnp.where(second, dot32(b, b), b)
        w_q[0:COARSE] = beside([-0.25 * a1, 0.25 * b1, jnp.where(second, 0.25 * group, 0.0)])
        w_q[COARSE:] = beside([a1, zero, jnp.where(second, a, 0.0)])

    def chain(it, ends):
        s_copy(it).wait_recv()
        force = tall(ends) - s_in[it]
        f_out[it] = force
        if it == 0:
            f_near().start()
            f_pair[0, core] = force
            f_near().wait_recv()
        else:

            @pl.when(chip < NY * NZ - 1)
            def _():
                f_far(0).start()
                f_far(1).start()

            @pl.when(chip > 0)
            def _():
                for c in (0, 1):
                    copy(f_out.at[1], f_pair.at[1, c], SEM_F + 2, SEM_F + 2 + c, sibling).wait_recv()

        t_all[it, yh] = f_pair[it, 1] + dot32(w_m[0], f_pair[it, 0])
        for k in (2, 1, 3):
            y_copy(it, k).start()
        for k in (1, 2, 3):
            copy(z_out.at[it], t_all.at[it, lax.rem(yh + NY - k, NY)], SEM_Y, SEM_Y + 3 * it + k - 1, sibling).wait_recv()
        both = dot32(w_y[...], jnp.concatenate([t_all[it, j] for j in range(NY)], axis=0))
        z_out[it] = both[COARSE:]
        for k in (4, 3, 5, 2, 6, 1, 7):

            @pl.when(z + k < NZ)
            def _(k=k):
                z_copy(it, k).start()

        if it == 1:

            @pl.when(tm < slices - 2)
            def _():
                copy(state, fin, SEM_END, SEM_END, at(lax.rem(tm + 2, slices))).start()

        for k in range(1, NZ):

            @pl.when(z >= k)
            def _(k=k):
                z_copy(it, k).wait_recv()

        before = both[0:COARSE] + dot32(w_z[...], jnp.concatenate([z_all[it, k] for k in range(NZ - 1)], axis=0))
        p_pair[it, core] = before
        p_copy(it).start()
        copy(z_out.at[it], p_pair.at[it, 1 - core], SEM_P + it, SEM_P + it, sibling).wait_recv()
        both = dot32(w_q[...], jnp.concatenate([p_pair[it, 0], p_pair[it, 1], f_pair[it, 0]], axis=0))
        mine = pick(both[0:COARSE], maps[0:1])
        q_out[it] = mine
        for k in (3, 1, 2):
            q_copy(it, k).start()
        for k in (2, 1, 3):
            q_copy(it, k).wait_recv()
        mean = (mine + q_all[it, 0]) + (q_all[it, 1] + q_all[it, 2])
        return wide(both[COARSE:] + pick(mean, maps[8:9]))

    sides = [restriction, orders, powers, y_weights, z_weights, q_weights, lambda: None, lambda: None]
    for n in range(SUB):
        ends = substep(n, sides[n])
    correction = chain(0, ends)
    raise_by = node_rows(prolong)
    trace = state[0:FACE, :] + dot32(raise_by[0:FACE], correction)
    sent[SUB] = trace
    halo(SUB).start()
    state[0:FACE, :] = trace
    state[FACE:, :] = state[FACE:, :] + dot32(raise_by[FACE:], correction)

    first_to_second = copy(cand, fin, SEM_END, SEM_END, sibling)

    @pl.when(tm == 0)
    def _():
        cand[...] = state[...]
        first_to_second.start()
        for c in range(COMP):
            fin[:, c * EL : (c + 1) * EL] = node_rows(guess, c * NODES)

    for n in range(SUB, 2 * SUB):
        ends = substep(n, functools.partial(send_starts, 1) if n == SUB else lambda: None)
    correction = chain(1, ends)
    added = dot32(raise_by, correction)

    @pl.when(tm > 0)
    def _():
        first_to_second.wait_recv()

    for c in range(COMP):
        for k, i in enumerate((3, 0, 1, 2)):
            rows = slice(k * FACE, (k + 1) * FACE)
            out[pl.ds(c * NODES + i, FACE, stride=4), :] = fin[rows, c * EL : (c + 1) * EL] + part(added[rows], c)

    for n in range(2 * SUB):
        halo(n).wait_send()
    f_near().wait_send()
    for it in range(ITERS):
        s_copy(it).wait_send()
        for k in (1, 2, 3):
            y_copy(it, k).wait_send()
            q_copy(it, k).wait_send()
        p_copy(it).wait_send()
        for k in range(1, NZ):

            @pl.when(z + k < NZ)
            def _(k=k):
                z_copy(it, k).wait_send()

    @pl.when(chip < NY * NZ - 1)
    def _():
        f_far(0).wait_send()
        f_far(1).wait_send()

    @pl.when(tm == 0)
    def _():
        first_to_second.wait_send()

    @pl.when(tm < slices - 2)
    def _():
        copy(state, fin, SEM_END, SEM_END + 0, sibling).wait_send()


def body(guess, deriv, viscous, jacobian, upwind, lift, restrict, prolong, coarse_self, coarse_group, neighbors, coarse_map):
    vmem = pl.BlockSpec(memory_space=pltpu.VMEM)
    smem = pl.BlockSpec(memory_space=pltpu.SMEM)

    def buffer(*shape):
        return pltpu.VMEM(shape, f32)

    result = pl.pallas_call(
        kernel,
        out_shape=jax.ShapeDtypeStruct((COMP * NODES, EL), f32),
        in_specs=[vmem, vmem, vmem, smem, smem, vmem, vmem, vmem, vmem, vmem, vmem, vmem],
        out_specs=vmem,
        scratch_shapes=[
            buffer(NODES, WIDE),
            buffer(NODES, WIDE),
            buffer(2 * SUB, FACE, WIDE),
            buffer(2 * SUB, FACE, WIDE),
            buffer(ITERS, COARSE, EL),
            buffer(ITERS, COARSE, EL),
            buffer(ITERS, COARSE, EL),
            buffer(ITERS, 2, COARSE, EL),
            buffer(ITERS, NY, COARSE, EL),
            buffer(ITERS, COARSE, EL),
            buffer(ITERS, NZ - 1, COARSE, EL),
            buffer(ITERS, 2, COARSE, EL),
            buffer(ITERS, COARSE, EL),
            buffer(ITERS, 3, COARSE, EL),
            buffer(NODES, WIDE),
            buffer(NODES, WIDE),
            pltpu.VMEM((2 * NODES, 3 * NODES), bf16),
            pltpu.VMEM((NODES, 3 * FACE), bf16),
            pltpu.VMEM((CNODES, 3 * NODES), bf16),
            pltpu.VMEM((CNODES, 3 * FACE), bf16),
            buffer(5, COARSE, COARSE),
            buffer(2 * COARSE, NY * COARSE),
            buffer(COARSE, (NZ - 1) * COARSE),
            buffer(2 * COARSE, 3 * COARSE),
            pltpu.VMEM((16, EL), jnp.int32),
            pltpu.SemaphoreType.DMA((SEMS,)),
            pltpu.SemaphoreType.DMA((SEMS,)),
        ],
        compiler_params=pltpu.CompilerParams(
            collective_id=0, has_side_effects=True, vmem_limit_bytes=32 * 2**20
        ),
        name="parareal",
    )(
        guess.reshape(COMP * NODES, EL), deriv, viscous, jacobian, upwind, lift, restrict, prolong,
        coarse_self, coarse_group, neighbors.reshape(1, EL), coarse_map.reshape(16, EL),
    )
    return result.reshape(1, COMP, NODES, EL)


def solution(mesh):
    return jax.shard_map(
        body,
        mesh=mesh,
        in_specs=(
            P("tm", None, None, "space"),
            P(), P(), P(), P(), P(), P(), P(), P(), P(),
            P("space"),
            P(),
        ),
        out_specs=P("tm", None, None, "space"),
        check_vma=False,
    )
```

profile of v0, /device:TPU:146, one launch (start us, length us, event | category | flops | bytes accessed | tf_op | source)
XLA Modules:
  0.0 116.8 jit_solution(4566364340826166685)
XLA Ops:
  0.0 0.0 copy-start.7
  0.0 0.0 copy-start.9
  0.0 0.0 copy-start.1
  0.0 0.0 copy-start.2
  0.0 0.8 copy.13.lift
  0.8 0.0 copy-start.5
  0.8 0.0 copy-start.6
  0.9 0.8 copy.14.prolong
  1.6 0.0 copy-done.7
  1.6 0.0 copy-done.9
  1.7 0.0 copy-done.1
  1.7 0.0 copy-done.2
  1.7 0.0 copy-done.5
  1.7 0.0 copy-done.6
  1.7 0.0 copy-start
  1.7 0.9 copy-done
  2.6 0.0 copy-start.3
  2.6 0.7 copy-done.3
  3.3 0.0 copy-start.4
  3.3 0.7 copy-done.4
  4.1 0.0 copy-start.8
  4.1 0.7 copy-done.8
  4.8 111.4 %parareal.1 = f32[320,128]{1,0:T(8,128)S(1)} custom-call(f32[320,128]{1,0:T(8,128)S(1)} %bitcast.5, f32[64,64]{1,0:T(8,128)S(1)} %copy-done.1, f32[64,64]{1,0:T(8,128)S(1)} %copy-done.2, f32[5,5]{1,0:T(8,128)S(1)} %copy-done.6, f32[5,5]{1,0:T(8,128)S(1)} %copy-done.7, f32[64,16]{1,0:T(8,128)S(1)} %copy.13.lift, f32[8,64]{1,0:T(8,128)S(1)} %copy-done.8, ...), custom_call_target="tpu_custom_call" | custom-call | tf_op jit(solution)/shard_map/parareal/pallas_call | solution.py:432
  116.2 0.7 copy.16
Async XLA Ops:
  0.0 1.6 %copy-start.7 = (f32[5,5]{1,0:T(8,128)S(1)}, f32[5,5]{1,0:T(8,128)}, u32[]{:S(2)}) copy-start(f32[5,5]{1,0:T(8,128)} %upwind.1) | copy-start | bytes 304
  0.0 1.6 %copy-start.9 = (s32[128]{0:T(128)S(1)}, s32[128]{0:T(128)}, u32[]{:S(2)}) copy-start(s32[128]{0:T(128)} %param.22) | copy-start | bytes 1540
  0.0 1.7 %copy-start.1 = (f32[64,64]{1,0:T(8,128)S(1)}, f32[64,64]{1,0:T(8,128)}, u32[]{:S(2)}) copy-start(f32[64,64]{1,0:T(8,128)} %deriv.1) | copy-start | bytes 49156
  0.0 1.7 %copy-start.2 = (f32[64,64]{1,0:T(8,128)S(1)}, f32[64,64]{1,0:T(8,128)}, u32[]{:S(2)}) copy-start(f32[64,64]{1,0:T(8,128)} %viscous.1) | copy-start | bytes 49156
  0.8 0.8 copy-start.5
  0.8 0.8 copy-start.6
  1.7 0.9 copy-start
  2.6 0.7 copy-start.3
  3.3 0.7 copy-start.4
  4.1 0.7 copy-start.8
where the time goes:
time: 117 us
  Pallas kernels  111 us (95%)
  local copies, waits for them, and re-layouts  5.36 us (5%)
    pallas_call x1, Pallas kernels, body(): pl.pallas_call(kernel, out_shape=jax.ShapeDtypeStruct((COMP * NODES, EL),...  111 us
    unnamed x23, local copies, waits for them, and re-layouts  5.36 us

commit v1 on v0

--- a/solution.py
+++ b/solution.py
@@ -25,8 +25,12 @@
 highest = lax.Precision.HIGHEST
 MESH = pl.DeviceIdType.MESH
 
-HALO = 0
-SEM_S = HALO + SUB * ITERS
+PAIRS = SUB // 2
+TRACE = 0
+TRACE2 = TRACE + PAIRS * ITERS
+AHEAD = TRACE2 + PAIRS * ITERS
+SEM_NB = AHEAD + PAIRS * ITERS
+SEM_S = SEM_NB + 1
 SEM_F = SEM_S + ITERS
 SEM_Y = SEM_F + 2 * ITERS
 SEM_Z = SEM_Y + 3 * ITERS
@@ -34,6 +38,7 @@
 SEM_Q = SEM_P + ITERS
 SEM_END = SEM_Q + 3 * ITERS
 SEMS = SEM_END + 1
+INPUTS = 12
 
 
 def iota(shape, dim):
@@ -100,12 +105,35 @@
 
 
 def kernel(
+    guess_in, deriv_in, viscous_in, jacobian_in, upwind_in, lift_in, restrict_in, prolong_in, self_in, group_in,
+    neighbors_in, coarse_map_in,
+    out,
     guess, deriv, viscous, jacobian, upwind, lift, restrict, prolong, self_ref, group_ref, neighbors, coarse_map,
-    out,
-    state, base, sent, landed, s_out, s_in, f_out, f_pair, t_all, z_out, z_all, p_pair, q_out, q_all, cand, fin,
+    state, base, trace_out, ahead_out, trace_in, trace2_in, ahead_in, nb_out, nb_in, s_out, s_in, f_out, f_pair, t_all, z_out, z_all, p_pair, q_out, q_all, cand, fin,
     gen3, lift3, rst3, rl3, w_m, w_y, w_z, w_q, maps,
-    ssem, rsem,
+    ssem, rsem, isem, ready,
 ):
+    loads = [
+        pltpu.make_async_copy(src, dst, isem.at[k])
+        for k, (src, dst) in enumerate(
+            [
+                (guess_in, guess),
+                (viscous_in, viscous),
+                (deriv_in, deriv),
+                (lift_in, lift),
+                (neighbors_in, neighbors),
+                (jacobian_in, jacobian),
+                (upwind_in, upwind),
+                (restrict_in, restrict),
+                (self_in, self_ref),
+                (group_in, group_ref),
+                (coarse_map_in, coarse_map),
+                (prolong_in, prolong),
+            ]
+        )
+    ]
+    for load in loads:
+        load.start()
     tm, sp = lax.axis_index("tm"), lax.axis_index("space")
     core, chip = lax.rem(tm, 2), tm // 2
     yh, z = lax.rem(chip, NY), chip // NY
@@ -135,8 +163,22 @@
             src_ref=src, dst_ref=dst, send_sem=ssem.at[send], recv_sem=rsem.at[recv], device_id=to, device_id_type=MESH
         )
 
-    def halo(n):
-        return copy(sent.at[n], landed.at[n], HALO + n, HALO + n, sp_at(1))
+    def trace_copy(n):
+        return copy(trace_out.at[n], trace_in.at[n], TRACE + n, TRACE + n, sp_at(1))
+
+    def trace2_copy(n):
+        return copy(trace_out.at[n], trace2_in.at[n], TRACE2 + n, TRACE2 + n, sp_at(2))
+
+    def ahead_copy(n):
+        return copy(ahead_out.at[n], ahead_in.at[n], AHEAD + n, AHEAD + n, sp_at(1))
+
+    def nb_copy():
+        return copy(nb_out, nb_in, SEM_NB, SEM_NB, sp_at(1))
+
+    def send_trace(n, trace):
+        trace_out[n] = trace
+        trace2_copy(n).start()
+        trace_copy(n).start()
 
     def s_copy(it):
         return copy(s_out.at[it], s_in.at[it], SEM_S + it, SEM_S + it, lower)
@@ -161,70 +203,164 @@
 
     z_all[...] = jnp.zeros_like(z_all)
     f_pair[...] = jnp.zeros_like(f_pair)
-
+    s_in[...] = jnp.zeros_like(s_in)
+
+    chips = NY * NZ
     barrier = pltpu.get_barrier_semaphore()
-    senders = [sp_at(-1), upper, sibling, chip_at(chip - 1, 0), chip_at(chip - 1, 1)]
-    senders += [y_at(-k) for k in (1, 2, 3)] + [z_at(-k) for k in range(1, NZ)] + [sp_at(-4 * k) for k in (1, 2, 3)]
-    for device in senders:
-        pl.semaphore_signal(barrier, inc=1, device_id=device, device_id_type=MESH)
-
+
+    def tell(semaphore, device):
+        pl.semaphore_signal(semaphore, inc=1, device_id=device, device_id_type=MESH)
+
+    for device in [sp_at(-1), sp_at(-2), sp_at(4), sp_at(8), sp_at(12), sibling]:
+        tell(barrier, device)
+
+    @pl.when(tm < slices - 1)
+    def _():
+        tell(barrier, upper)
+
+    @pl.when(chip < chips - 1)
+    def _():
+        tell(barrier, chip_at(chip + 1, 0))
+        tell(barrier, chip_at(chip + 1, 1))
+
+    for k in range(1, NY):
+
+        @pl.when(yh + k < NY)
+        def _(k=k):
+            tell(barrier, y_at(k))
+
+    for k in range(1, NZ):
+
+        @pl.when(z + k < NZ)
+        def _(k=k):
+            tell(barrier, z_at(k))
+
+    heard = 6 + lax.min(tm, 1) + 2 * lax.min(chip, 1) + yh + z
+
+    def report():
+        @pl.when(chip > 0)
+        def _():
+            tell(ready.at[2], chip_at(chip - 1, 0))
+            tell(ready.at[2], chip_at(chip - 1, 1))
+
+        for k in range(1, NY):
+
+            @pl.when(yh - k >= 0)
+            def _(k=k):
+                tell(ready.at[0], y_at(-k))
+
+        for k in range(1, NZ):
+
+            @pl.when(z - k >= 0)
+            def _(k=k):
+                tell(ready.at[1], z_at(-k))
+
+    def hear(which, count):
+        @pl.when(count > 0)
+        def _():
+            pl.semaphore_wait(ready.at[which], count)
+
+    rows, cols = iota((NODES, NODES), 0), iota((NODES, NODES), 1)
+    reorder = jnp.where(node_place(cols, rows), 1.0, 0.0)
+
+    def reordered(flipped):
+        return lax.dot_general(
+            reorder, flipped, (((1,), (1,)), ((), ())), precision=highest, preferred_element_type=f32
+        )
+
+    loads[0].wait()
     for c in range(COMP):
         state[:, c * EL : (c + 1) * EL] = node_rows(guess, c * NODES)
-    sent[0] = state[0:FACE, :]
-
-    index = neighbors[...] % EL
-    own = (neighbors[...] // EL) == jnp.broadcast_to(sp, (1, EL))
-    own = jnp.broadcast_to(own, (FACE, EL))
+    for load in loads[1:7]:
+        load.wait()
+
+    def sides(numbers, place):
+        here = (numbers // EL) == jnp.broadcast_to(place, (1, EL))
+        return numbers % EL, jnp.broadcast_to(here, (FACE, EL))
+
+    index, own = sides(neighbors[...], sp)
+    nb_out[...] = jnp.broadcast_to(neighbors[...].astype(f32), (8, EL))
+
+    pl.semaphore_wait(barrier, heard)
+    send_trace(0, state[0:FACE, :])
+    nb_copy().start()
+    report()
 
     volume = jnp.concatenate([node_rows(viscous), node_rows(deriv)], axis=0) * STEP
     gen3[...] = spread3(volume, node_place)
-    lift_rows = node_rows(lift) * STEP
+    lift_rows = reordered(lift[...]) * STEP
     lift3[...] = spread3(lift_rows, same)
 
-    pl.semaphore_wait(barrier, len(senders))
-    halo(0).start()
-
-    def substep(n, side):
-        last = n % SUB == SUB - 1
-        v = state[...]
+    def volume_part(v, dest):
         yz = dot(gen3[...], stack3(v))
-        plus, minus = v[0:FACE], v[FACE : 2 * FACE]
-        inner = [pick(part(plus, d), index) - part(minus, d) for d in range(COMP)]
         for c in range(COMP):
             total = part(v, c) + part(yz[0:NODES], c)
             for d in range(COMP):
                 total = total - jacobian[c, d] * part(yz[NODES:], d)
-            base[:, c * EL : (c + 1) * EL] = total
-        if last:
-            coarse_base = dot(rst3[...], stack3(base[...]))
-        side()
-        halo(n).wait_recv()
-        jump = [jnp.where(own, inner[d], pick(landed[n, :, d * EL : (d + 1) * EL], index) - part(minus, d)) for d in range(COMP)]
+            dest[:, c * EL : (c + 1) * EL] = total
+
+    def faces(jump):
         mixed = []
         for c in range(COMP):
             total = upwind[c, 0] * jump[0]
             for d in range(1, COMP):
                 total = total + upwind[c, d] * jump[d]
             mixed.append(total)
-        faces = stack3(jnp.concatenate(mixed, axis=1))
+        return stack3(jnp.concatenate(mixed, axis=1))
+
+    def pair(n, side):
+        last = n % PAIRS == PAIRS - 1
+        v = state[...]
+        volume_part(v, base)
+        minus = [part(v[FACE : 2 * FACE], d) for d in range(COMP)]
+        inner = [pick(part(v[0:FACE], d), index) for d in range(COMP)]
+        known = faces([jnp.where(own, inner[d], 0.0) - minus[d] for d in range(COMP)])
+        ahead_out[n] = base[0:FACE, :] + dot(lift3[0:FACE, :], known)
+        ahead_copy(n).start()
+        side()
+        if n == 0:
+            nb_copy().wait_recv()
+        trace_copy(n).wait_recv()
+        jump = [
+            jnp.where(own, inner[d], pick(trace_in[n, :, d * EL : (d + 1) * EL], index)) - minus[d] for d in range(COMP)
+        ]
+        v = base[...] + dot(lift3[...], faces(jump))
+        volume_part(v, base)
         if last:
-            ends = coarse_base + dot(rl3[...], faces)
-            state[...] = base[...] + dot(lift3[...], faces)
+            coarse_base = dot(rst3[...], stack3(base[...]))
+        minus = [part(v[FACE : 2 * FACE], d) for d in range(COMP)]
+        inner = [pick(part(v[0:FACE], d), index) for d in range(COMP)]
+        index_before, own_before = sides(nb_in[0:1, :].astype(jnp.int32), lax.rem(sp + parts - 1, parts))
+        trace2_copy(n).wait_recv()
+        jump = [
+            jnp.where(own_before, 0.0, pick(trace2_in[n, :, d * EL : (d + 1) * EL], index_before)) for d in range(COMP)
+        ]
+        missing = dot(lift3[0:FACE, :], faces(jump))
+        ahead_copy(n).wait_recv()
+        before = ahead_in[n] + missing
+        jump = [jnp.where(own, inner[d], pick(part(before, d), index)) - minus[d] for d in range(COMP)]
+        entering = faces(jump)
+        if last:
+            ends = coarse_base + dot(rl3[...], entering)
+            state[...] = base[...] + dot(lift3[...], entering)
             return ends
-        trace = base[0:FACE, :] + dot(lift3[0:FACE, :], faces)
-        sent[n + 1] = trace
-        halo(n + 1).start()
+        trace = base[0:FACE, :] + dot(lift3[0:FACE, :], entering)
+        send_trace(n + 1, trace)
         state[0:FACE, :] = trace
-        state[FACE:, :] = base[FACE:, :] + dot(lift3[FACE:, :], faces)
+        state[FACE:, :] = base[FACE:, :] + dot(lift3[FACE:, :], entering)
 
     def send_starts(it):
         s_out[it] = tall(dot(rst3[...], stack3(state[...])))
-        s_copy(it).start()
+
+        @pl.when(tm > 0)
+        def _():
+            s_copy(it).start()
 
     def restriction():
+        for load in loads[7:]:
+            load.wait()
         full = restrict[...]
         rst3[...] = spread3(full, node_place)
-        rows, cols = iota((NODES, NODES), 0), iota((NODES, NODES), 1)
         moved = dot32(full, jnp.where(node_place(rows, cols), 1.0, 0.0))
         rl3[...] = spread3(dot32(moved, lift_rows), same)
         send_starts(0)
@@ -301,7 +437,10 @@
         w_q[COARSE:] = beside([a1, zero, jnp.where(second, a, 0.0)])
 
     def chain(it, ends):
-        s_copy(it).wait_recv()
+        @pl.when(tm < slices - 1)
+        def _():
+            s_copy(it).wait_recv()
+
         force = tall(ends) - s_in[it]
         f_out[it] = force
         if it == 0:
@@ -309,8 +448,9 @@
             f_pair[0, core] = force
             f_near().wait_recv()
         else:
-
-            @pl.when(chip < NY * NZ - 1)
+            hear(2, 2 * lax.min(chips - 1 - chip, 1))
+
+            @pl.when(chip < chips - 1)
             def _():
                 f_far(0).start()
                 f_far(1).start()
@@ -321,12 +461,16 @@
                     copy(f_out.at[1], f_pair.at[1, c], SEM_F + 2, SEM_F + 2 + c, sibling).wait_recv()
 
         t_all[it, yh] = f_pair[it, 1] + dot32(w_m[0], f_pair[it, 0])
+        if it == 0:
+            hear(0, NY - 1 - yh)
         for k in (2, 1, 3):
             y_copy(it, k).start()
         for k in (1, 2, 3):
             copy(z_out.at[it], t_all.at[it, lax.rem(yh + NY - k, NY)], SEM_Y, SEM_Y + 3 * it + k - 1, sibling).wait_recv()
         both = dot32(w_y[...], jnp.concatenate([t_all[it, j] for j in range(NY)], axis=0))
         z_out[it] = both[COARSE:]
+        if it == 0:
+            hear(1, NZ - 1 - z)
         for k in (4, 3, 5, 2, 6, 1, 7):
 
             @pl.when(z + k < NZ)
@@ -359,14 +503,22 @@
         mean = (mine + q_all[it, 0]) + (q_all[it, 1] + q_all[it, 2])
         return wide(both[COARSE:] + pick(mean, maps[8:9]))
 
-    sides = [restriction, orders, powers, y_weights, z_weights, q_weights, lambda: None, lambda: None]
-    for n in range(SUB):
-        ends = substep(n, sides[n])
+    def after(*steps):
+        for step in steps:
+            step()
+
+    tasks = [
+        functools.partial(after, restriction, orders),
+        functools.partial(after, powers, y_weights),
+        functools.partial(after, z_weights),
+        functools.partial(after, q_weights),
+    ]
+    for n in range(PAIRS):
+        ends = pair(n, tasks[n])
     correction = chain(0, ends)
-    raise_by = node_rows(prolong)
+    raise_by = reordered(prolong[...])
     trace = state[0:FACE, :] + dot32(raise_by[0:FACE], correction)
-    sent[SUB] = trace
-    halo(SUB).start()
+    send_trace(PAIRS, trace)
     state[0:FACE, :] = trace
     state[FACE:, :] = state[FACE:, :] + dot32(raise_by[FACE:], correction)
 
@@ -379,8 +531,8 @@
         for c in range(COMP):
             fin[:, c * EL : (c + 1) * EL] = node_rows(guess, c * NODES)
 
-    for n in range(SUB, 2 * SUB):
-        ends = substep(n, functools.partial(send_starts, 1) if n == SUB else lambda: None)
+    for n in range(PAIRS, 2 * PAIRS):
+        ends = pair(n, functools.partial(send_starts, 1) if n == PAIRS else after)
     correction = chain(1, ends)
     added = dot32(raise_by, correction)
 
@@ -393,11 +545,18 @@
             rows = slice(k * FACE, (k + 1) * FACE)
             out[pl.ds(c * NODES + i, FACE, stride=4), :] = fin[rows, c * EL : (c + 1) * EL] + part(added[rows], c)
 
-    for n in range(2 * SUB):
-        halo(n).wait_send()
+    nb_copy().wait_send()
+    for n in range(2 * PAIRS):
+        trace_copy(n).wait_send()
+        trace2_copy(n).wait_send()
+        ahead_copy(n).wait_send()
     f_near().wait_send()
     for it in range(ITERS):
-        s_copy(it).wait_send()
+
+        @pl.when(tm > 0)
+        def _(it=it):
+            s_copy(it).wait_send()
+
         for k in (1, 2, 3):
             y_copy(it, k).wait_send()
             q_copy(it, k).wait_send()
@@ -408,7 +567,7 @@
             def _(k=k):
                 z_copy(it, k).wait_send()
 
-    @pl.when(chip < NY * NZ - 1)
+    @pl.when(chip < chips - 1)
     def _():
         f_far(0).wait_send()
         f_far(1).wait_send()
@@ -423,8 +582,7 @@
 
 
 def body(guess, deriv, viscous, jacobian, upwind, lift, restrict, prolong, coarse_self, coarse_group, neighbors, coarse_map):
-    vmem = pl.BlockSpec(memory_space=pltpu.VMEM)
-    smem = pl.BlockSpec(memory_space=pltpu.SMEM)
+    hbm = pl.BlockSpec(memory_space=pltpu.HBM)
 
     def buffer(*shape):
         return pltpu.VMEM(shape, f32)
@@ -432,13 +590,30 @@
     result = pl.pallas_call(
         kernel,
         out_shape=jax.ShapeDtypeStruct((COMP * NODES, EL), f32),
-        in_specs=[vmem, vmem, vmem, smem, smem, vmem, vmem, vmem, vmem, vmem, vmem, vmem],
-        out_specs=vmem,
+        in_specs=[hbm] * INPUTS,
+        out_specs=pl.BlockSpec(memory_space=pltpu.VMEM),
         scratch_shapes=[
+            buffer(COMP * NODES, EL),
+            buffer(NODES, NODES),
+            buffer(NODES, NODES),
+            pltpu.SMEM((COMP, COMP), f32),
+            pltpu.SMEM((COMP, COMP), f32),
+            buffer(FACE, NODES),
+            buffer(CNODES, NODES),
+            buffer(CNODES, NODES),
+            buffer(COARSE, COARSE),
+            buffer(COARSE, COARSE),
+            pltpu.VMEM((1, EL), jnp.int32),
+            pltpu.VMEM((16, EL), jnp.int32),
             buffer(NODES, WIDE),
             buffer(NODES, WIDE),
-            buffer(2 * SUB, FACE, WIDE),
-            buffer(2 * SUB, FACE, WIDE),
+            buffer(2 * PAIRS, FACE, WIDE),
+            buffer(2 * PAIRS, FACE, WIDE),
+            buffer(2 * PAIRS, FACE, WIDE),
+            buffer(2 * PAIRS, FACE, WIDE),
+            buffer(2 * PAIRS, FACE, WIDE),
+            buffer(8, EL),
+            buffer(8, EL),
             buffer(ITERS, COARSE, EL),
             buffer(ITERS, COARSE, EL),
             buffer(ITERS, COARSE, EL),
@@ -462,13 +637,15 @@
             pltpu.VMEM((16, EL), jnp.int32),
             pltpu.SemaphoreType.DMA((SEMS,)),
             pltpu.SemaphoreType.DMA((SEMS,)),
+            pltpu.SemaphoreType.DMA((INPUTS,)),
+            pltpu.SemaphoreType.REGULAR((3,)),
         ],
         compiler_params=pltpu.CompilerParams(
-            collective_id=0, has_side_effects=True, vmem_limit_bytes=32 * 2**20
+            collective_id=0, has_side_effects=True, vmem_limit_bytes=60 * 2**20
         ),
         name="parareal",
     )(
-        guess.reshape(COMP * NODES, EL), deriv, viscous, jacobian, upwind, lift, restrict, prolong,
+        guess.reshape(COMP * NODES, EL), deriv, viscous, jacobian, upwind, lift.T, restrict, prolong.T,
         coarse_self, coarse_group, neighbors.reshape(1, EL), coarse_map.reshape(16, EL),
     )
     return result.reshape(1, COMP, NODES, EL)

time: 117 us -> 94.9 us (0.81)
  the two profiles are of different devices: /device:TPU:146 before, /device:TPU:257 now
where the time goes in v1:
time: 94.9 us; the launch traced here: 94.8 us
  Pallas kernels  93.2 us (98%)
  local copies, waits for them, and re-layouts  1.59 us (2%)
    pallas_call x1, Pallas kernels, body(): pl.pallas_call(kernel, out_shape=jax.ShapeDtypeStruct((COMP * NODES, EL),...  93.2 us

profile of v1, /device:TPU:257, one launch (start us, length us, event | category | flops | bytes accessed | tf_op | source)
XLA Modules:
  0.0 94.8 jit_solution(16639034704297532015)
XLA Ops:
  0.0 93.2 %parareal.1 = f32[320,128]{1,0:T(8,128)} custom-call(f32[320,128]{1,0:T(8,128)} %bitcast.7, f32[64,64]{1,0:T(8,128)} %deriv_in.1, f32[64,64]{1,0:T(8,128)} %viscous_in.1, f32[5,5]{1,0:T(8,128)} %jacobian_in.1, f32[5,5]{1,0:T(8,128)} %upwind_in.1, f32[16,64]{1,0:T(8,128)} %bitcast.8, f32[8,64]{1,0:T(8,128)} %restrict_in.1, f32[8,64]{1,0:T(8,128)} %bitcast.10, ...), custom_call_target="tpu_custom_call" | custom-call | tf_op jit(solution)/shard_map/parareal/pallas_call | solution.py:590
  93.2 1.6 %copy.14 = f32[1,5,64,128]{3,2,1,0:T(8,128)} copy(f32[1,5,64,128]{3,2,1,0:T(8,128)} %bitcast.6) | data formatting | bytes 327680

commit v2 on v1

--- a/solution.py
+++ b/solution.py
@@ -32,9 +32,11 @@
 SEM_NB = AHEAD + PAIRS * ITERS
 SEM_S = SEM_NB + 1
 SEM_F = SEM_S + ITERS
-SEM_Y = SEM_F + 2 * ITERS
-SEM_Z = SEM_Y + 3 * ITERS
-SEM_P = SEM_Z + 7 * ITERS
+SEM_LATE = SEM_F + ITERS
+SEM_Y = SEM_LATE + 1
+SEM_Z = SEM_Y + NY * ITERS
+SEM_PRE = SEM_Z + (NZ - 1) * ITERS
+SEM_P = SEM_PRE + ITERS
 SEM_Q = SEM_P + ITERS
 SEM_END = SEM_Q + 3 * ITERS
 SEMS = SEM_END + 1
@@ -51,6 +53,11 @@
 
 def dot32(a, b):
     return jnp.dot(a, b, precision=highest, preferred_element_type=f32)
+
+
+def dot3(weights, x):
+    high, low = halves(x)
+    return dot(weights[0], high) + (dot(weights[1], high) + dot(weights[0], low))
 
 
 def halves(x):
@@ -109,8 +116,8 @@
     neighbors_in, coarse_map_in,
     out,
     guess, deriv, viscous, jacobian, upwind, lift, restrict, prolong, self_ref, group_ref, neighbors, coarse_map,
-    state, base, trace_out, ahead_out, trace_in, trace2_in, ahead_in, nb_out, nb_in, s_out, s_in, f_out, f_pair, t_all, z_out, z_all, p_pair, q_out, q_all, cand, fin,
-    gen3, lift3, rst3, rl3, w_m, w_y, w_z, w_q, maps,
+    state, base, trace_out, ahead_out, trace_in, trace2_in, ahead_in, nb_out, nb_in, s_out, s_in, f_out, f_pair, f_late, t_out, t_all, z_out, z_all, pre, late, q_out, q_all, cand, fin,
+    gen3, lift3, rst3, rl3, w_m, w_t, w_y, w_z, w_q, maps,
     ssem, rsem, isem, ready,
 ):
     loads = [
@@ -142,14 +149,19 @@
     def at(t=None, s=None):
         return {"tm": tm if t is None else t, "space": sp if s is None else s}
 
+    other = 1 - core
+
     def chip_at(q, c):
-        return at(2 * lax.rem(q + NY * NZ, NY * NZ) + c)
+        return at(2 * q + c)
 
     def y_at(k):
-        return at((z * NY + lax.rem(yh + k + NY, NY)) * 2 + core)
+        return at((z * NY + lax.rem(yh + k + NY, NY)) * 2 + other)
 
     def z_at(k):
-        return at(lax.rem(tm + 2 * NY * k + slices, slices))
+        return at(2 * (chip + NY * k) + other)
+
+    def edge_at(target):
+        return at(2 * ((z + 1) * NY + target) + other)
 
     def sp_at(k):
         return at(None, lax.rem(sp + k + parts, parts))
@@ -183,26 +195,53 @@
     def s_copy(it):
         return copy(s_out.at[it], s_in.at[it], SEM_S + it, SEM_S + it, lower)
 
-    def f_near():
-        return copy(f_out.at[0], f_pair.at[0, core], SEM_F, SEM_F, sibling)
-
-    def f_far(c):
-        return copy(f_out.at[1], f_pair.at[1, core], SEM_F + 2 + c, SEM_F + 2 + core, chip_at(chip + 1, c))
+    def f_copy(it):
+        return copy(f_out.at[it], f_pair.at[it, core], SEM_F + it, SEM_F + it, sibling)
+
+    def late_copy():
+        return copy(f_pair.at[1, 0], f_late, SEM_LATE, SEM_LATE, chip_at(chip + 1, core))
 
     def y_copy(it, k):
-        return copy(t_all.at[it, yh], t_all.at[it, yh], SEM_Y + 3 * it + k - 1, SEM_Y + 3 * it + k - 1, y_at(k))
+        if it == 0:
+            slot, to = yh, y_at(k)
+        else:
+            slot = lax.rem(yh + 1, NY)
+            to = at((chip // NY * NY + lax.rem(yh + k, NY) + NY * (yh // (NY - 1))) * 2 + other)
+        return copy(t_out.at[it], t_all.at[it, slot], SEM_Y + NY * it + k, SEM_Y + NY * it + slot, to)
+
+    def y_sends(it, act):
+        for k in (2, 1, 3, 0):
+            if it == 0:
+                if k > 0:
+                    act(y_copy(it, k))
+            else:
+                allowed = (yh == NY - 1) & (z < NZ - 1)
+                if k > 0:
+                    allowed = allowed | (yh < NY - 1)
+
+                @pl.when(allowed)
+                def _(k=k):
+                    act(y_copy(it, k))
 
     def z_copy(it, k):
-        return copy(z_out.at[it], z_all.at[it, k - 1], SEM_Z + 7 * it + k - 1, SEM_Z + 7 * it + k - 1, z_at(k))
+        sem = SEM_Z + (NZ - 1) * it + k - 1
+        return copy(z_out.at[it], z_all.at[it, k - 1], sem, sem, z_at(k))
+
+    def pre_copy(it):
+        return copy(pre.at[it, other], pre.at[it, other], SEM_PRE + it, SEM_PRE + it, sibling)
 
     def p_copy(it):
-        return copy(p_pair.at[it, core], p_pair.at[it, core], SEM_P + it, SEM_P + it, sibling)
+        return copy(late.at[it, core], late.at[it, core], SEM_P + it, SEM_P + it, sibling)
 
     def q_copy(it, k):
-        return copy(q_out.at[it], q_all.at[it, k - 1], SEM_Q + 3 * it + k - 1, SEM_Q + 3 * it + k - 1, sp_at(4 * k))
+        sem = SEM_Q + 3 * it + k - 1
+        to = at(tm + 1 - 2 * core, lax.rem(sp + 4 * k, parts))
+        return copy(q_out.at[it], q_all.at[it, k - 1], sem, sem, to)
 
     z_all[...] = jnp.zeros_like(z_all)
-    f_pair[...] = jnp.zeros_like(f_pair)
+    t_all[1, 0] = jnp.zeros((COARSE, EL), f32)
+    f_late[...] = jnp.zeros_like(f_late)
+    late[...] = jnp.zeros_like(late)
     s_in[...] = jnp.zeros_like(s_in)
 
     chips = NY * NZ
@@ -211,7 +250,8 @@
     def tell(semaphore, device):
         pl.semaphore_signal(semaphore, inc=1, device_id=device, device_id_type=MESH)
 
-    for device in [sp_at(-1), sp_at(-2), sp_at(4), sp_at(8), sp_at(12), sibling]:
+    peers = [at(tm + 1 - 2 * core, lax.rem(sp + 4 * k, parts)) for k in (1, 2, 3)]
+    for device in [sp_at(-1), sp_at(-2), sibling] + peers:
         tell(barrier, device)
 
     @pl.when(tm < slices - 1)
@@ -220,8 +260,7 @@
 
     @pl.when(chip < chips - 1)
     def _():
-        tell(barrier, chip_at(chip + 1, 0))
-        tell(barrier, chip_at(chip + 1, 1))
+        tell(barrier, chip_at(chip + 1, core))
 
     for k in range(1, NY):
 
@@ -235,13 +274,23 @@
         def _(k=k):
             tell(barrier, z_at(k))
 
-    heard = 6 + lax.min(tm, 1) + 2 * lax.min(chip, 1) + yh + z
+    last_y, first_y = yh // (NY - 1), 1 - yh // (NY - 1)
+
+    @pl.when((yh == NY - 1) & (z < NZ - 1))
+    def _():
+        for target in range(NY - 1):
+            tell(barrier, edge_at(target))
+
+    heard = 6 + lax.min(tm, 1) + lax.min(chip, 1) + yh + z + first_y * lax.min(z, 1)
 
     def report():
         @pl.when(chip > 0)
         def _():
-            tell(ready.at[2], chip_at(chip - 1, 0))
-            tell(ready.at[2], chip_at(chip - 1, 1))
+            tell(ready.at[2], chip_at(chip - 1, core))
+
+        @pl.when((yh < NY - 1) & (z > 0))
+        def _():
+            tell(ready.at[3], at(2 * (z * NY - 1) + other))
 
         for k in range(1, NY):
 
@@ -381,24 +430,25 @@
     eye = jnp.where(iota(small, 0) == iota(small, 1), 1.0, 0.0)
     zero = jnp.zeros(small, f32)
 
+    def put(ref, value):
+        high, low = halves(value)
+        ref[0] = high
+        ref[1] = low
+
+    def beside(blocks):
+        return jnp.concatenate(blocks, axis=1)
+
     def powers():
-        m = self_ref[...] + jnp.where(second, group_ref[...], 0.0)
-        w = dot32(m, m)
-        w2 = dot32(w, w)
-        w_m[0] = m
-        w_m[1] = w
-        w_m[2] = w2
-        w_m[3] = dot32(w2, w)
-        w_m[4] = dot32(w2, w2)
-
-    def beside(blocks):
-        count = len(blocks)
-        total = None
-        for k, block in enumerate(blocks):
-            rows, cols = iota((COARSE, COARSE * count), 0), iota((COARSE, COARSE * count), 1)
-            term = dot32(block, jnp.where(cols - COARSE * k == rows, 1.0, 0.0))
-            total = term if total is None else total + term
-        return total
+        a = self_ref[...]
+        b = a + group_ref[...]
+        put(w_t, jnp.concatenate([a, b], axis=0))
+        for j, m in enumerate((a, b)):
+            w = dot32(m, m)
+            w2 = dot32(w, w)
+            w_m[j, 0] = w
+            w_m[j, 1] = w2
+            w_m[j, 2] = dot32(w2, w)
+            w_m[j, 3] = dot32(w2, w2)
 
     def by_yh(choices):
         place = jnp.broadcast_to(yh, small)
@@ -408,33 +458,31 @@
         return value
 
     def y_weights():
-        w, w2, w3 = w_m[1], w_m[2], w_m[3]
-        w_y[0:COARSE] = beside(
-            [
-                by_yh([zero, eye, w, w2]),
-                by_yh([zero, zero, eye, w]),
-                by_yh([zero, zero, zero, eye]),
-                zero,
-            ]
+        w, w2, w3 = [jnp.where(second, w_m[0, j], w_m[1, j]) for j in range(3)]
+        before = beside(
+            [by_yh([zero, eye, w, w2]), by_yh([zero, zero, eye, w]), by_yh([zero, zero, zero, eye]), zero]
         )
-        w_y[COARSE:] = beside([w3, w2, w, eye])
+        put(w_y, jnp.concatenate([before, beside([w3, w2, w, eye])], axis=0))
 
     def z_weights():
-        w8 = w_m[4]
-        weight = by_yh([eye, w_m[1], w_m[2], w_m[3]])
+        w, w2, w3, w8 = [jnp.where(second, w_m[1, j], w_m[0, j]) for j in range(4)]
+        weight = by_yh([eye, w, w2, w3])
         weights = [weight]
         for k in range(NZ - 2):
             weight = dot32(weight, w8)
             weights.append(weight)
-        w_z[...] = beside(weights)
+        put(w_z, beside(weights))
 
     def q_weights():
         a, group = self_ref[...], group_ref[...]
         b = a + group
-        a1 = jnp.where(second, dot32(a, a), a)
-        b1 = jnp.where(second, dot32(b, b), b)
-        w_q[0:COARSE] = beside([-0.25 * a1, 0.25 * b1, jnp.where(second, 0.25 * group, 0.0)])
-        w_q[COARSE:] = beside([a1, zero, jnp.where(second, a, 0.0)])
+        aa, bb = w_m[0, 0], w_m[1, 0]
+        even = beside([-0.25 * a, 0.25 * b, zero])
+        odd = beside([-0.25 * aa, 0.25 * bb, 0.25 * group])
+        even_own, odd_own = beside([a, zero, zero]), beside([aa, zero, a])
+        here = jnp.broadcast_to(core, odd.shape) == 1
+        mine, sent, own = jnp.where(here, odd, even), jnp.where(here, even, odd), jnp.where(here, odd_own, even_own)
+        put(w_q, jnp.concatenate([mine, sent, own], axis=0))
 
     def chain(it, ends):
         @pl.when(tm < slices - 1)
@@ -443,31 +491,43 @@
 
         force = tall(ends) - s_in[it]
         f_out[it] = force
+        f_copy(it).start()
+        f_pair[it, core] = force
+        copy(f_out.at[it], f_pair.at[it, other], SEM_F + it, SEM_F + it, sibling).wait_recv()
+        both = dot3(w_t, f_pair[it, 0])
+        first, other_chain = f_pair[it, 1] + both[0:COARSE], f_pair[it, 1] + both[COARSE:]
+        is_second = jnp.broadcast_to(core, (COARSE, EL)) == 1
+        t_out[it] = jnp.where(is_second, other_chain, first)
+        kept = jnp.where(is_second, first, other_chain)
         if it == 0:
-            f_near().start()
-            f_pair[0, core] = force
-            f_near().wait_recv()
+            hear(0, NY - 1 - yh)
+            t_all[it, yh] = kept
         else:
-            hear(2, 2 * lax.min(chips - 1 - chip, 1))
+            hear(3, (NY - 1) * last_y * lax.min(NZ - 1 - z, 1))
+
+            @pl.when(yh < NY - 1)
+            def _():
+                t_all[it, lax.rem(yh + 1, NY)] = kept
+
+        y_sends(it, lambda c: c.start())
+        if it == 1:
+            hear(2, lax.min(chips - 1 - chip, 1))
 
             @pl.when(chip < chips - 1)
             def _():
-                f_far(0).start()
-                f_far(1).start()
-
-            @pl.when(chip > 0)
-            def _():
-                for c in (0, 1):
-                    copy(f_out.at[1], f_pair.at[1, c], SEM_F + 2, SEM_F + 2 + c, sibling).wait_recv()
-
-        t_all[it, yh] = f_pair[it, 1] + dot32(w_m[0], f_pair[it, 0])
-        if it == 0:
-            hear(0, NY - 1 - yh)
-        for k in (2, 1, 3):
-            y_copy(it, k).start()
-        for k in (1, 2, 3):
-            copy(z_out.at[it], t_all.at[it, lax.rem(yh + NY - k, NY)], SEM_Y, SEM_Y + 3 * it + k - 1, sibling).wait_recv()
-        both = dot32(w_y[...], jnp.concatenate([t_all[it, j] for j in range(NY)], axis=0))
+                late_copy().start()
+
+        for j in range(NY):
+            if it == 0:
+                awaited = yh != j
+            else:
+                awaited = yh + 1 != j if j else z > 0
+
+            @pl.when(awaited)
+            def _(j=j):
+                copy(t_out.at[it], t_all.at[it, j], SEM_Y, SEM_Y + NY * it + j, sibling).wait_recv()
+
+        both = dot3(w_y, jnp.concatenate([t_all[it, j] for j in range(NY)], axis=0))
         z_out[it] = both[COARSE:]
         if it == 0:
             hear(1, NZ - 1 - z)
@@ -477,31 +537,47 @@
             def _(k=k):
                 z_copy(it, k).start()
 
+        pre[it, other] = both[0:COARSE]
+        pre_copy(it).start()
         if it == 1:
 
             @pl.when(tm < slices - 2)
             def _():
-                copy(state, fin, SEM_END, SEM_END, at(lax.rem(tm + 2, slices))).start()
-
-        for k in range(1, NZ):
-
-            @pl.when(z >= k)
-            def _(k=k):
-                z_copy(it, k).wait_recv()
-
-        before = both[0:COARSE] + dot32(w_z[...], jnp.concatenate([z_all[it, k] for k in range(NZ - 1)], axis=0))
-        p_pair[it, core] = before
-        p_copy(it).start()
-        copy(z_out.at[it], p_pair.at[it, 1 - core], SEM_P + it, SEM_P + it, sibling).wait_recv()
-        both = dot32(w_q[...], jnp.concatenate([p_pair[it, 0], p_pair[it, 1], f_pair[it, 0]], axis=0))
-        mine = pick(both[0:COARSE], maps[0:1])
-        q_out[it] = mine
+                copy(state, fin, SEM_END, SEM_END, at(tm + 2)).start()
+
+        @pl.when(z > 0)
+        def _():
+            for k in range(1, NZ):
+
+                @pl.when(z >= k)
+                def _(k=k):
+                    z_copy(it, k).wait_recv()
+
+            late[it, core] = dot3(w_z, jnp.concatenate([z_all[it, k] for k in range(NZ - 1)], axis=0))
+            p_copy(it).start()
+
+        copy(z_out.at[it], pre.at[it, core], SEM_PRE, SEM_PRE + it, sibling).wait_recv()
+        if it == 1:
+
+            @pl.when(chip > 0)
+            def _():
+                copy(z_out.at[it], f_late, SEM_LATE, SEM_LATE, sibling).wait_recv()
+
+        @pl.when(z > 0)
+        def _():
+            copy(z_out.at[it], late.at[it, other], SEM_P, SEM_P + it, sibling).wait_recv()
+
+        before = [pre[it, j] + late[it, j] for j in (0, 1)]
+        stacked = jnp.concatenate(before + [f_pair[it, 0] if it == 0 else f_late[...]], axis=0)
+        parts3 = dot3(w_q, stacked)
+        q_out[it] = pick(parts3[COARSE : 2 * COARSE], maps[0:1])
         for k in (3, 1, 2):
             q_copy(it, k).start()
+        mine = pick(parts3[0:COARSE], maps[0:1])
         for k in (2, 1, 3):
             q_copy(it, k).wait_recv()
         mean = (mine + q_all[it, 0]) + (q_all[it, 1] + q_all[it, 2])
-        return wide(both[COARSE:] + pick(mean, maps[8:9]))
+        return wide(parts3[2 * COARSE :] + pick(mean, maps[8:9]))
 
     def after(*steps):
         for step in steps:
@@ -509,9 +585,9 @@
 
     tasks = [
         functools.partial(after, restriction, orders),
-        functools.partial(after, powers, y_weights),
-        functools.partial(after, z_weights),
-        functools.partial(after, q_weights),
+        powers,
+        z_weights,
+        functools.partial(after, y_weights, q_weights),
     ]
     for n in range(PAIRS):
         ends = pair(n, tasks[n])
@@ -550,27 +626,31 @@
         trace_copy(n).wait_send()
         trace2_copy(n).wait_send()
         ahead_copy(n).wait_send()
-    f_near().wait_send()
     for it in range(ITERS):
 
         @pl.when(tm > 0)
         def _(it=it):
             s_copy(it).wait_send()
 
+        f_copy(it).wait_send()
+        y_sends(it, lambda c: c.wait_send())
+        pre_copy(it).wait_send()
         for k in (1, 2, 3):
-            y_copy(it, k).wait_send()
             q_copy(it, k).wait_send()
-        p_copy(it).wait_send()
+
+        @pl.when(z > 0)
+        def _(it=it):
+            p_copy(it).wait_send()
+
         for k in range(1, NZ):
 
             @pl.when(z + k < NZ)
-            def _(k=k):
+            def _(k=k, it=it):
                 z_copy(it, k).wait_send()
 
     @pl.when(chip < chips - 1)
     def _():
-        f_far(0).wait_send()
-        f_far(1).wait_send()
+        late_copy().wait_send()
 
     @pl.when(tm == 0)
     def _():
@@ -618,9 +698,12 @@
             buffer(ITERS, COARSE, EL),
             buffer(ITERS, COARSE, EL),
             buffer(ITERS, 2, COARSE, EL),
+            buffer(COARSE, EL),
+            buffer(ITERS, COARSE, EL),
             buffer(ITERS, NY, COARSE, EL),
             buffer(ITERS, COARSE, EL),
             buffer(ITERS, NZ - 1, COARSE, EL),
+            buffer(ITERS, 2, COARSE, EL),
             buffer(ITERS, 2, COARSE, EL),
             buffer(ITERS, COARSE, EL),
             buffer(ITERS, 3, COARSE, EL),
@@ -630,15 +713,16 @@
             pltpu.VMEM((NODES, 3 * FACE), bf16),
             pltpu.VMEM((CNODES, 3 * NODES), bf16),
             pltpu.VMEM((CNODES, 3 * FACE), bf16),
-            buffer(5, COARSE, COARSE),
-            buffer(2 * COARSE, NY * COARSE),
-            buffer(COARSE, (NZ - 1) * COARSE),
-            buffer(2 * COARSE, 3 * COARSE),
+            buffer(2, 4, COARSE, COARSE),
+            pltpu.VMEM((2, 2 * COARSE, COARSE), bf16),
+            pltpu.VMEM((2, 2 * COARSE, NY * COARSE), bf16),
+            pltpu.VMEM((2, COARSE, (NZ - 1) * COARSE), bf16),
+            pltpu.VMEM((2, 3 * COARSE, 3 * COARSE), bf16),
             pltpu.VMEM((16, EL), jnp.int32),
             pltpu.SemaphoreType.DMA((SEMS,)),
             pltpu.SemaphoreType.DMA((SEMS,)),
             pltpu.SemaphoreType.DMA((INPUTS,)),
-            pltpu.SemaphoreType.REGULAR((3,)),
+            pltpu.SemaphoreType.REGULAR((4,)),
         ],
         compiler_params=pltpu.CompilerParams(
             collective_id=0, has_side_effects=True, vmem_limit_bytes=60 * 2**20

time: 94.9 us -> 91.2 us (0.961)
  Pallas kernels: 93.2 us -> 89.5 us
    pallas_call x1, Pallas kernels: 93.2 us -> 89.5 us  [body(): pl.pallas_call(kernel, out_shape=jax.ShapeDtypeStruct((COMP * NODES, EL),...]
where the time goes in v2:
time: 91.2 us; the launch traced here: 91.1 us
  Pallas kernels  89.5 us (98%)
  local copies, waits for them, and re-layouts  1.59 us (2%)
    pallas_call x1, Pallas kernels, body(): pl.pallas_call(kernel, out_shape=jax.ShapeDtypeStruct((COMP * NODES, EL),...  89.5 us

profile of v2, /device:TPU:257, one launch (start us, length us, event | category | flops | bytes accessed | tf_op | source)
XLA Modules:
  0.0 91.1 jit_solution(15870695170242044835)
XLA Ops:
  0.0 89.5 %parareal.1 = f32[320,128]{1,0:T(8,128)} custom-call(f32[320,128]{1,0:T(8,128)} %bitcast.7, f32[64,64]{1,0:T(8,128)} %deriv_in.1, f32[64,64]{1,0:T(8,128)} %viscous_in.1, f32[5,5]{1,0:T(8,128)} %jacobian_in.1, f32[5,5]{1,0:T(8,128)} %upwind_in.1, f32[16,64]{1,0:T(8,128)} %bitcast.8, f32[8,64]{1,0:T(8,128)} %restrict_in.1, f32[8,64]{1,0:T(8,128)} %bitcast.10, ...), custom_call_target="tpu_custom_call" | custom-call | tf_op jit(solution)/shard_map/parareal/pallas_call | solution.py:670
  89.5 1.6 %copy.14 = f32[1,5,64,128]{3,2,1,0:T(8,128)} copy(f32[1,5,64,128]{3,2,1,0:T(8,128)} %bitcast.6) | data formatting | bytes 327680

commit v3 on v2

--- a/solution.py
+++ b/solution.py
@@ -70,6 +70,11 @@
     return jnp.concatenate([high, high, low], axis=0)
 
 
+def stack_short(x):
+    high = x.astype(bf16).astype(f32)
+    return jnp.concatenate([high, high, x - high], axis=0).astype(bf16)
+
+
 def spread3(x, place):
     depth = x.shape[1]
     rows, cols = iota((depth, 3 * depth), 0), iota((depth, 3 * depth), 1)
@@ -117,7 +122,7 @@
     out,
     guess, deriv, viscous, jacobian, upwind, lift, restrict, prolong, self_ref, group_ref, neighbors, coarse_map,
     state, base, trace_out, ahead_out, trace_in, trace2_in, ahead_in, nb_out, nb_in, s_out, s_in, f_out, f_pair, f_late, t_out, t_all, z_out, z_all, pre, late, q_out, q_all, cand, fin,
-    gen3, lift3, rst3, rl3, w_m, w_t, w_y, w_z, w_q, maps,
+    gen3, lift3, rst3, rl3, pro3, w_m, w_t, w_y, w_z, w_q, maps,
     ssem, rsem, isem, ready,
 ):
     loads = [
@@ -333,7 +338,6 @@
     pl.semaphore_wait(barrier, heard)
     send_trace(0, state[0:FACE, :])
     nb_copy().start()
-    report()
 
     volume = jnp.concatenate([node_rows(viscous), node_rows(deriv)], axis=0) * STEP
     gen3[...] = spread3(volume, node_place)
@@ -410,6 +414,7 @@
             load.wait()
         full = restrict[...]
         rst3[...] = spread3(full, node_place)
+        pro3[...] = spread3(reordered(prolong[...]), same)
         moved = dot32(full, jnp.where(node_place(rows, cols), 1.0, 0.0))
         rl3[...] = spread3(dot32(moved, lift_rows), same)
         send_starts(0)
@@ -531,7 +536,7 @@
         z_out[it] = both[COARSE:]
         if it == 0:
             hear(1, NZ - 1 - z)
-        for k in (4, 3, 5, 2, 6, 1, 7):
+        for k in range(1, NZ):
 
             @pl.when(z + k < NZ)
             def _(k=k):
@@ -584,7 +589,7 @@
             step()
 
     tasks = [
-        functools.partial(after, restriction, orders),
+        functools.partial(after, report, restriction, orders),
         powers,
         z_weights,
         functools.partial(after, y_weights, q_weights),
@@ -592,11 +597,11 @@
     for n in range(PAIRS):
         ends = pair(n, tasks[n])
     correction = chain(0, ends)
-    raise_by = reordered(prolong[...])
-    trace = state[0:FACE, :] + dot32(raise_by[0:FACE], correction)
+    rising = stack_short(correction)
+    trace = state[0:FACE, :] + dot(pro3[0:FACE, :], rising)
     send_trace(PAIRS, trace)
     state[0:FACE, :] = trace
-    state[FACE:, :] = state[FACE:, :] + dot32(raise_by[FACE:], correction)
+    state[FACE:, :] = state[FACE:, :] + dot(pro3[FACE:, :], rising)
 
     first_to_second = copy(cand, fin, SEM_END, SEM_END, sibling)
 
@@ -610,7 +615,7 @@
     for n in range(PAIRS, 2 * PAIRS):
         ends = pair(n, functools.partial(send_starts, 1) if n == PAIRS else after)
     correction = chain(1, ends)
-    added = dot32(raise_by, correction)
+    added = dot(pro3[...], stack_short(correction))
 
     @pl.when(tm > 0)
     def _():
@@ -713,6 +718,7 @@
             pltpu.VMEM((NODES, 3 * FACE), bf16),
             pltpu.VMEM((CNODES, 3 * NODES), bf16),
             pltpu.VMEM((CNODES, 3 * FACE), bf16),
+            pltpu.VMEM((NODES, 3 * CNODES), bf16),
             buffer(2, 4, COARSE, COARSE),
             pltpu.VMEM((2, 2 * COARSE, COARSE), bf16),
             pltpu.VMEM((2, 2 * COARSE, NY * COARSE), bf16),

time: 91.2 us -> 89.8 us (0.985)
  Pallas kernels: 89.5 us -> 88 us
    pallas_call x1, Pallas kernels: 89.5 us -> 88 us  [body(): pl.pallas_call(kernel, out_shape=jax.ShapeDtypeStruct((COMP * NODES, EL),...]
where the time goes in v3:
time: 89.8 us; the launch traced here: 89.6 us
  Pallas kernels  88 us (98%)
  local copies, waits for them, and re-layouts  1.59 us (2%)
    pallas_call x1, Pallas kernels, body(): pl.pallas_call(kernel, out_shape=jax.ShapeDtypeStruct((COMP * NODES, EL),...  88 us

profile of v3, /device:TPU:257, one launch (start us, length us, event | category | flops | bytes accessed | tf_op | source)
XLA Modules:
  0.0 89.6 jit_solution(770292950261412337)
XLA Ops:
  0.0 88.0 %parareal.1 = f32[320,128]{1,0:T(8,128)} custom-call(f32[320,128]{1,0:T(8,128)} %bitcast.7, f32[64,64]{1,0:T(8,128)} %deriv_in.1, f32[64,64]{1,0:T(8,128)} %viscous_in.1, f32[5,5]{1,0:T(8,128)} %jacobian_in.1, f32[5,5]{1,0:T(8,128)} %upwind_in.1, f32[16,64]{1,0:T(8,128)} %bitcast.8, f32[8,64]{1,0:T(8,128)} %restrict_in.1, f32[8,64]{1,0:T(8,128)} %bitcast.10, ...), custom_call_target="tpu_custom_call" | custom-call | tf_op jit(solution)/shard_map/parareal/pallas_call | solution.py:675
  88.0 1.6 %copy.14 = f32[1,5,64,128]{3,2,1,0:T(8,128)} copy(f32[1,5,64,128]{3,2,1,0:T(8,128)} %bitcast.6) | data formatting | bytes 327680

commit v4 on v3

--- a/solution.py
+++ b/solution.py
@@ -544,11 +544,6 @@
 
         pre[it, other] = both[0:COARSE]
         pre_copy(it).start()
-        if it == 1:
-
-            @pl.when(tm < slices - 2)
-            def _():
-                copy(state, fin, SEM_END, SEM_END, at(tm + 2)).start()
 
         @pl.when(z > 0)
         def _():
@@ -578,6 +573,11 @@
         q_out[it] = pick(parts3[COARSE : 2 * COARSE], maps[0:1])
         for k in (3, 1, 2):
             q_copy(it, k).start()
+        if it == 1:
+
+            @pl.when(tm < slices - 2)
+            def _():
+                copy(state, fin, SEM_END, SEM_END, at(tm + 2)).start()
         mine = pick(parts3[0:COARSE], maps[0:1])
         for k in (2, 1, 3):
             q_copy(it, k).wait_recv()

time: 89.8 us -> 89.2 us (level)
  the two profiles are of different devices: /device:TPU:257 before, /device:TPU:896 now
where the time goes in v4:
time: 89.2 us; the launch traced here: 89.1 us
  Pallas kernels  87.5 us (98%)
  local copies, waits for them, and re-layouts  1.59 us (2%)
    pallas_call x1, Pallas kernels, body(): pl.pallas_call(kernel, out_shape=jax.ShapeDtypeStruct((COMP * NODES, EL),...  87.5 us

profile of v4, /device:TPU:896, one launch (start us, length us, event | category | flops | bytes accessed | tf_op | source)
XLA Modules:
  0.0 89.1 jit_solution(12468650829927988128)
XLA Ops:
  0.0 87.5 %parareal.1 = f32[320,128]{1,0:T(8,128)} custom-call(f32[320,128]{1,0:T(8,128)} %bitcast.7, f32[64,64]{1,0:T(8,128)} %deriv_in.1, f32[64,64]{1,0:T(8,128)} %viscous_in.1, f32[5,5]{1,0:T(8,128)} %jacobian_in.1, f32[5,5]{1,0:T(8,128)} %upwind_in.1, f32[16,64]{1,0:T(8,128)} %bitcast.8, f32[8,64]{1,0:T(8,128)} %restrict_in.1, f32[8,64]{1,0:T(8,128)} %bitcast.10, ...), custom_call_target="tpu_custom_call" | custom-call | tf_op jit(solution)/shard_map/parareal/pallas_call | solution.py:675
  87.5 1.6 %copy.14 = f32[1,5,64,128]{3,2,1,0:T(8,128)} copy(f32[1,5,64,128]{3,2,1,0:T(8,128)} %bitcast.6) | data formatting | bytes 327680

commit v5 on v4

--- a/solution.py
+++ b/solution.py
@@ -395,8 +395,7 @@
         entering = faces(jump)
         if last:
             ends = coarse_base + dot(rl3[...], entering)
-            state[...] = base[...] + dot(lift3[...], entering)
-            return ends
+            return ends, entering
         trace = base[0:FACE, :] + dot(lift3[0:FACE, :], entering)
         send_trace(n + 1, trace)
         state[0:FACE, :] = trace
@@ -489,7 +488,7 @@
         mine, sent, own = jnp.where(here, odd, even), jnp.where(here, even, odd), jnp.where(here, odd_own, even_own)
         put(w_q, jnp.concatenate([mine, sent, own], axis=0))
 
-    def chain(it, ends):
+    def chain(it, ends, entering):
         @pl.when(tm < slices - 1)
         def _():
             s_copy(it).wait_recv()
@@ -497,6 +496,7 @@
         force = tall(ends) - s_in[it]
         f_out[it] = force
         f_copy(it).start()
+        state[...] = base[...] + dot(lift3[...], entering)
         f_pair[it, core] = force
         copy(f_out.at[it], f_pair.at[it, other], SEM_F + it, SEM_F + it, sibling).wait_recv()
         both = dot3(w_t, f_pair[it, 0])
@@ -596,7 +596,7 @@
     ]
     for n in range(PAIRS):
         ends = pair(n, tasks[n])
-    correction = chain(0, ends)
+    correction = chain(0, *ends)
     rising = stack_short(correction)
     trace = state[0:FACE, :] + dot(pro3[0:FACE, :], rising)
     send_trace(PAIRS, trace)
@@ -614,7 +614,7 @@
 
     for n in range(PAIRS, 2 * PAIRS):
         ends = pair(n, functools.partial(send_starts, 1) if n == PAIRS else after)
-    correction = chain(1, ends)
+    correction = chain(1, *ends)
     added = dot(pro3[...], stack_short(correction))
 
     @pl.when(tm > 0)

time: 89.2 us -> 89.5 us (level)
  no operation moved by 1% of the time
where the time goes in v5:
time: 89.5 us; the launch traced here: 89.3 us
  Pallas kernels  87.7 us (98%)
  local copies, waits for them, and re-layouts  1.59 us (2%)
    pallas_call x1, Pallas kernels, body(): pl.pallas_call(kernel, out_shape=jax.ShapeDtypeStruct((COMP * NODES, EL),...  87.7 us

profile of v5, /device:TPU:896, one launch (start us, length us, event | category | flops | bytes accessed | tf_op | source)
XLA Modules:
  0.0 89.3 jit_solution(9396633695980156625)
XLA Ops:
  0.0 87.7 %parareal.1 = f32[320,128]{1,0:T(8,128)} custom-call(f32[320,128]{1,0:T(8,128)} %bitcast.7, f32[64,64]{1,0:T(8,128)} %deriv_in.1, f32[64,64]{1,0:T(8,128)} %viscous_in.1, f32[5,5]{1,0:T(8,128)} %jacobian_in.1, f32[5,5]{1,0:T(8,128)} %upwind_in.1, f32[16,64]{1,0:T(8,128)} %bitcast.8, f32[8,64]{1,0:T(8,128)} %restrict_in.1, f32[8,64]{1,0:T(8,128)} %bitcast.10, ...), custom_call_target="tpu_custom_call" | custom-call | tf_op jit(solution)/shard_map/parareal/pallas_call | solution.py:675
  87.7 1.6 %copy.14 = f32[1,5,64,128]{3,2,1,0:T(8,128)} copy(f32[1,5,64,128]{3,2,1,0:T(8,128)} %bitcast.6) | data formatting | bytes 327680
